TPU v7x, 256 devices: a whole 4x4x8 slice. The times are simulated.
256 devices in a mesh: tm: 128 (over z, y, x), seq: 2 (over core).
Axes of the slice: x: 4, y: 4, z: 8, core: 2. Of those that a mesh axis runs over, the one named last changes fastest.
Arguments:
- noise: float32 [8, 128, 64], P(None, 'seq'), may hold values from -6 to 6
- step_size: float32 [128], P('tm'), may hold values from 0.05 to 0.15
- step_ids: int32 [128], P('tm'), may hold values from 0 to 49, as said below
- mod_table: float32 [50, 3, 3072], replicated, may hold values from -3 to 3
- w_in: bfloat16 [64, 3072], replicated
- w_qkv: bfloat16 [3072, 3, 1536], P(None, None, 'seq'), may hold values from -0.109375 to 0.109375
- w_out: bfloat16 [1536, 3072], replicated, may hold values from -1.25 to 1.25
- w_final: bfloat16 [3072, 64], replicated, may hold values from -0.109375 to 0.109375
- text_keys: bfloat16 [256, 1536], P(None, 'seq'), may hold values from -6 to 6
- text_values: bfloat16 [256, 1536], P(None, 'seq'), may hold values from -6 to 6
Outputs:
- trajectory: float32 [128, 128, 64], P('tm', 'seq')
Inputs may be any that keep to these rules, and one draw needn't show every extreme that they name: `step_ids`: for each block b, the levels of entries k * 8 + b fall strictly as k rises; the first step of every block is at level 49 and the last at level 0.
All inputs are finite; a program needn't handle non-finite values.
Results may differ from a plain program's by a relative error of at most 0.0035.
Values may be sent and summed in bfloat16 or wider, within the bound.
A program may use at most 128 MiB of HBM per device.

v0:
```python
import jax
import jax.numpy as jnp
from jax import lax
from jax.sharding import PartitionSpec as P

HD = 128
ITERS = 2


epsilon = 1e-06


def carried_in(value, axis, join, neutral):
    count, mine = (lax.axis_size(axis), lax.axis_index(axis))
    pieces = lax.all_gather(value, axis)
    total = jnp.full_like(value, 0) + jnp.asarray(neutral, value.dtype)

    def lap(position, total):
        longer = join(total, pieces[position])
        return jnp.where(position < mine, longer, total)

    return lax.fori_loop(0, count - 1, lap, total)


def layer_norm(values):
    average = jnp.mean(values, axis=-1, keepdims=True)
    centred = values - average
    spread = jnp.mean(centred * centred, axis=-1, keepdims=True)
    return centred * lax.rsqrt(spread + epsilon)


def head_norm(values):
    return values * lax.rsqrt(jnp.mean(values * values, axis=-1, keepdims=True) + epsilon)


def add_terms(earlier, later):
    return earlier + later


def per_device(
    noise, step_size, step_ids, mod_table, w_in, w_qkv, w_out, w_final, text_keys, text_values
):
    step_count = step_size.shape[0]
    block_count = noise.shape[0]
    time_index = lax.axis_index("tm")
    block_index = time_index % block_count
    own_noise = lax.dynamic_index_in_dim(noise, block_index, 0, keepdims=False)
    tok_local, channels = own_noise.shape
    model_width = w_in.shape[1]
    heads_local = text_keys.shape[1] // HD
    level_count = mod_table.shape[0]
    text_count = text_keys.shape[0]
    text_normed = head_norm(
        text_keys.astype(jnp.float32).reshape(text_count, heads_local, HD)
    ).astype(jnp.bfloat16)
    text_heads = text_values.reshape(text_count, heads_local, HD)
    qkv_local = w_qkv.reshape(model_width, 3 * heads_local * HD)
    one_hot = (step_ids[:, None] == jnp.arange(level_count, dtype=jnp.int32)[None, :]).astype(
        jnp.float32
    )
    modulation = jnp.dot(
        one_hot, mod_table.reshape(level_count, 3 * model_width), precision=lax.Precision.HIGHEST
    )
    modulation = modulation.reshape(step_count, 3, model_width)
    shift_term = modulation[:, 0][None]
    scale_term = modulation[:, 1][None]
    gate_term = modulation[:, 2][None]
    scale_factor = HD ** (-0.5)
    latent = own_noise[None]
    trajectory = latent
    for sweep in range(ITERS):
        hidden = jnp.einsum(
            "stc,cd->tsd", latent.astype(jnp.bfloat16), w_in, preferred_element_type=jnp.float32
        )
        normed = (layer_norm(hidden) * (1.0 + scale_term) + shift_term).astype(jnp.bfloat16)
        projected = jnp.einsum(
            "tsd,de->tse",
            lax.all_gather(normed, "seq", axis=0, tiled=True),
            qkv_local,
            preferred_element_type=jnp.float32,
        )
        rows_all = projected.shape[0]
        projected = projected.reshape(rows_all, step_count, 3, heads_local, HD)
        queries = head_norm(projected[:, :, 0]).astype(jnp.bfloat16)
        own_keys = head_norm(projected[:, :, 1]).astype(jnp.bfloat16)
        own_values = projected[:, :, 2].astype(jnp.bfloat16)
        own_scores = (
            jnp.einsum("qshd,kshd->shqk", queries, own_keys, preferred_element_type=jnp.float32)
            * scale_factor
        )
        text_scores = (
            jnp.einsum("qshd,khd->shqk", queries, text_normed, preferred_element_type=jnp.float32)
            * scale_factor
        )
        own_exp = jnp.exp(own_scores)
        text_exp = jnp.exp(text_scores)
        totals = jnp.sum(own_exp, axis=-1, keepdims=True) + jnp.sum(
            text_exp, axis=-1, keepdims=True
        )
        own_weights = (own_exp / totals).astype(jnp.bfloat16)
        text_weights = (text_exp / totals).astype(jnp.bfloat16)
        attended = jnp.einsum(
            "shqk,kshd->qshd", own_weights, own_values, preferred_element_type=jnp.float32
        )
        attended = attended + jnp.einsum(
            "shqk,khd->qshd", text_weights, text_heads, preferred_element_type=jnp.float32
        )
        attended = attended.astype(jnp.bfloat16).reshape(rows_all, step_count, heads_local * HD)
        head_start = lax.axis_index("seq") * (heads_local * HD)
        my_rows = lax.dynamic_slice_in_dim(w_out, head_start, heads_local * HD, 0)
        projection = lax.psum_scatter(
            jnp.einsum("tsh,hd->tsd", attended, my_rows, preferred_element_type=jnp.float32),
            "seq",
            scatter_dimension=0,
            tiled=True,
        )
        mixed_rows = hidden + gate_term * projection
        final_normed = layer_norm(mixed_rows).astype(jnp.bfloat16)
        velocity = jnp.einsum(
            "tsd,dc->stc", final_normed, w_final, preferred_element_type=jnp.float32
        )
        drifts = step_size[:, None, None] * velocity
        running = jnp.cumsum(drifts, axis=0)
        device_total = running[-1].reshape(tok_local * channels)
        block_slot = (jnp.arange(block_count, dtype=jnp.int32) == block_index).astype(jnp.float32)
        placed = block_slot[:, None] * device_total[None, :]
        scanned = carried_in(placed, "tm", add_terms, jnp.zeros_like(placed))
        earlier = lax.dynamic_index_in_dim(scanned, block_index, 0, keepdims=False)
        earlier = earlier.reshape(tok_local, channels)
        trajectory = own_noise[None] + (earlier[None] + running)
        latent = own_noise[None] + (earlier[None] + (running - drifts))
    return trajectory


def solution(mesh):
    placed = (
        P(None, "seq", None),
        P("tm"),
        P("tm"),
        P(),
        P(),
        P(None, None, "seq"),
        P(),
        P(),
        P(None, "seq"),
        P(None, "seq"),
    )
    return jax.shard_map(
        per_device, mesh=mesh, in_specs=placed, out_specs=P("tm", "seq", None), check_vma=False
    )
```

profile of v0, /device:TPU:226, one launch (start us, length us, event | category | flops | bytes accessed | tf_op | source)
XLA Modules:
  0.0 666.1 jit_solution(5650801174499411374)
XLA Ops:
  6.5 2.9 copy.40
  10.0 2.5 copy.75
  12.5 3.1 reshape.514
  16.2 1.8 fusion.10
  18.7 1.1 fusion.76
  20.3 2.4 all_gather.14
  22.6 18.6 %copy.41 = bf16[3072,3,768]{0,2,1:T(8,128)(2,1)} copy(bf16[3072,3,768]{2,0,1:T(8,128)(2,1)} %param.19) | data formatting | bytes 28311552 | tf_op args[5]
  41.3 7.1 %convolution_bitcast_fusion.1 = f32[128,1,3,6,128]{0,4,3,2,1:T(8,128)S(1)} fusion(bf16[3,6,128,3072]{3,2,1,0:T(8,128)(2,1)} %bitcast.213, bf16[128,1,3072]{2,0,1:T(8,128)(2,1)S(1)} %all_gather.14), kind=kOutput, calls=%fused_computation.11 | convolution fusion | flops 1811939328 | bytes 16121856 | tf_op jit(solution)/shard_map/tsd,de->tse/dot_general | solution.py:76
  50.7 1.9 copy.48
  53.4 1.3 convolution_bitcast_fusion.3
  54.9 4.3 fusion.4
  60.0 14.2 %reduce-scatter.3.cloned.1.call-done = f32[64,1,3072]{2,0,1:T(8,128)} async-done(((f32[128,1,3072]{2,0,1:T(8,128)}), f32[64,1,3072]{2,0,1:T(8,128)}) %reduce-scatter.3.cloned.1.call-update) | async-done | bytes 786448 | tf_op jit(solution)/shard_map/reduce_scatter | solution.py:111
  74.2 1.3 fusion.74
  77.0 151.5 %all-gather.3.cloned.1.call-done = f32[128,8,4096]{2,1,0:T(8,128)} async-done(((f32[1,8,4096]{2,1,0:T(8,128)}), f32[128,8,4096]{2,1,0:T(8,128)}) %all-gather.3.cloned.1.call-update) | async-done | bytes 16777232 | tf_op jit(solution)/shard_map/all_gather | solution.py:15
  228.6 123.1 %while.28 = (s32[]{:T(128)}, f32[8,4096]{1,0:T(8,128)S(1)}, s32[]{:T(128)}, f32[128,8,4096]{2,1,0:T(8,128)}, s32[]{:T(128)}, /*index=5*/s32[]{:T(128)}) while((s32[]{:T(128)}, f32[8,4096]{1,0:T(8,128)S(1)}, s32[]{:T(128)}, f32[128,8,4096]{2,1,0:T(8,128)}, s32[]{:T(128)}, /*index=5*/s32[]{:T(128)}) %tuple.71), condition=%wide.region_11.12_spmd.clone, body=%wide.region_10.11_spmd.clone.sunk | while | flops 98308 | bytes 393309 | solution.py:22
  351.8 1.1 fusion.79
  353.4 2.5 all_gather.16
  356.0 7.2 %convolution_bitcast_fusion = f32[128,1,3,6,128]{0,4,3,2,1:T(8,128)S(1)} fusion(bf16[3,6,128,3072]{3,2,1,0:T(8,128)(2,1)} %bitcast.214, bf16[128,1,3072]{2,0,1:T(8,128)(2,1)S(1)} %all_gather.16), kind=kOutput, calls=%fused_computation.10 | convolution fusion | flops 1811939328 | bytes 16121856 | tf_op jit(solution)/shard_map/tsd,de->tse/dot_general | solution.py:76
  365.4 2.0 fusion.7
  367.4 13.9 %reduce-scatter.5.cloned.1.call-done = f32[64,1,3072]{2,0,1:T(8,128)} async-done(((f32[128,1,3072]{2,0,1:T(8,128)}), f32[64,1,3072]{2,0,1:T(8,128)}) %reduce-scatter.5.cloned.1.call-update) | async-done | bytes 786448 | tf_op jit(solution)/shard_map/reduce_scatter | solution.py:111
  381.3 1.3 fusion.73
  384.1 150.8 %all-gather.5.cloned.1.call-done = f32[128,8,4096]{2,1,0:T(8,128)} async-done(((f32[1,8,4096]{2,1,0:T(8,128)}), f32[128,8,4096]{2,1,0:T(8,128)}) %all-gather.5.cloned.1.call-update) | async-done | bytes 16777232 | tf_op jit(solution)/shard_map/all_gather | solution.py:15
  534.9 123.1 %while.29 = (s32[]{:T(128)}, f32[8,4096]{1,0:T(8,128)S(1)}, s32[]{:T(128)}, f32[128,8,4096]{2,1,0:T(8,128)}, s32[]{:T(128)}, /*index=5*/s32[]{:T(128)}) while((s32[]{:T(128)}, f32[8,4096]{1,0:T(8,128)S(1)}, s32[]{:T(128)}, f32[128,8,4096]{2,1,0:T(8,128)}, s32[]{:T(128)}, /*index=5*/s32[]{:T(128)}) %tuple.74), condition=%wide.region_22.23_spmd.clone, body=%wide.region_21.22_spmd.clone.sunk | while | flops 98308 | bytes 393309 | solution.py:22
  658.1 1.4 add_add_fusion
  (336 shorter events, 251.1 us)
Async XLA Ops:
  6.5 12.1 %copy-start = (bf16[64,3072]{1,0:T(8,128)(2,1)S(1)}, bf16[64,3072]{1,0:T(8,128)(2,1)}, u32[]{:S(2)}) copy-start(bf16[64,3072]{1,0:T(8,128)(2,1)} %param.18) | copy-start | bytes 1179652
  6.5 67.7 %reduce-scatter.3.cloned.1.call-start = ((), (), s32[]{:S(2)}) async-start(), calls=%async_computation.2 | async-start | bytes 2359296 | tf_op jit(solution)/shard_map/reduce_scatter | solution.py:111
  18.6 4.0 copy-start.5
  41.3 7.2 %copy-start.2 = (bf16[256,768]{1,0:T(8,128)(2,1)S(1)}, bf16[256,768]{1,0:T(8,128)(2,1)}, u32[]{:S(2)}) copy-start(bf16[256,768]{1,0:T(8,128)(2,1)} %param.22) | copy-start | bytes 1179652
  48.8 1.0 copy-start.8
  52.7 2.0 copy-start.4
  54.9 19.3 %copy-start.7 = (f32[1,1,3072]{2,0,1:T(1,128)S(1)}, f32[1,1,3072]{2,0,1:T(1,128)}, u32[]{:S(2)}) copy-start(f32[1,1,3072]{2,0,1:T(1,128)} %get-tuple-element.219) | copy-start | bytes 36868
  59.2 16.6 %copy-start.1 = (bf16[3072,64]{0,1:T(8,128)(2,1)S(1)}, bf16[3072,64]{0,1:T(8,128)(2,1)}, u32[]{:S(2)}) copy-start(bf16[3072,64]{0,1:T(8,128)(2,1)} %param.21) | copy-start | bytes 1179652
  59.2 169.3 %all-gather.3.cloned.1.call-start = ((), (), s32[]{:S(2)}) async-start(), calls=%async_computation.3 | async-start | bytes 16908288 | tf_op jit(solution)/shard_map/all_gather | solution.py:15
  77.0 304.4 %reduce-scatter.5.cloned.1.call-start = ((), (), s32[]{:S(2)}) async-start(), calls=%async_computation.4 | async-start | bytes 2359296 | tf_op jit(solution)/shard_map/reduce_scatter | solution.py:111
  228.6 124.7 %copy-start.6 = (f32[1,1,3072]{2,0,1:T(1,128)S(1)}, f32[1,1,3072]{2,0,1:T(1,128)}, u32[]{:S(2)}) copy-start(f32[1,1,3072]{2,0,1:T(1,128)} %copy-done.5) | copy-start | bytes 36868
  356.0 7.4 %copy-start.9 = (f32[256,6]{0,1:T(8,128)S(1)}, f32[256,6]{0,1:T(8,128)}, u32[]{:S(2)}) copy-start(f32[256,6]{0,1:T(8,128)} %copy-done.8) | copy-start | bytes 18436
  356.0 8.0 %copy-start.3 = (bf16[256,768]{0,1:T(8,128)(2,1)S(1)}, bf16[256,768]{0,1:T(8,128)(2,1)}, u32[]{:S(2)}) copy-start(bf16[256,768]{0,1:T(8,128)(2,1)} %copy.48) | copy-start | bytes 1179652
  356.0 8.5 %slice-start = ((s8[9437184]{0:T(1024)(128)(4,1)}), s8[4194304]{0:T(1024)(128)(4,1)S(1)}, s32[]{:S(2)}) async-start(s8[9437184]{0:T(1024)(128)(4,1)} %bitcast.216), calls=%async_computation.6 | async-start | bytes 8388608
  356.0 8.5 %slice-start.1 = ((s8[9437184]{0:T(1024)(128)(4,1)}), s8[1048576]{0:T(1024)(128)(4,1)S(1)}, s32[]{:S(2)}) async-start(s8[9437184]{0:T(1024)(128)(4,1)} %bitcast.216), calls=%async_computation.7 | async-start | bytes 2097152
  363.2 2.2 slice-start.2
  367.4 167.5 %all-gather.5.cloned.1.call-start = ((), (), s32[]{:S(2)}) async-start(), calls=%async_computation.5 | async-start | bytes 16908288 | tf_op jit(solution)/shard_map/all_gather | solution.py:15
Sparse Core Ops, SparseCore 0:
  59.4 14.8 reduce-scatter.2
  78.6 149.9 all-gather.2
  367.5 13.7 reduce-scatter.4
  384.9 149.9 all-gather.4
where the time goes:
time: 677 us; the launch traced here: 666 us
  waiting for transfers between devices  331 us (49%)
  other arithmetic  248 us (37%)
  local copies, waits for them, and re-layouts  31.7 us (5%)
  matrix products  29.8 us (4%)
  between operations  14.9 us (2%)
    all_gather x2, waiting for transfers between devices, carried_in(): pieces = lax.all_gather(value, axis)  302 us
    select_n x254, other arithmetic, lap(): return jnp.where(position < mine, longer, total)  241 us
    reduce_scatter x2, waiting for transfers between devices, per_device(): lax.psum_scatter(jnp.einsum('tsh,hd->tsd', attended, my_rows, preferred_e...  28.1 us
    unnamed x32, local copies, waits for them, and re-layouts  27.6 us
    dot_general x2, matrix products, per_device(): jnp.einsum('tsd,de->tse', lax.all_gather(normed, 'seq', axis=0, tiled=Tru...  14.3 us
  transfers between devices with their start and end apart: 4, of which 4 were waited for; matrix products, arithmetic and copies ran while one was open for 0% of the time, Pallas kernels for 0%

commit v1 on v0

v1 whole, which is shorter than its diff:
```python
import functools
import math

import jax
import jax.numpy as jnp
from jax import lax
from jax.experimental import pallas as pl
from jax.experimental.pallas import tpu as pltpu
from jax.sharding import PartitionSpec as P

HD = 128
ITERS = 2
EPS = 1e-06
MESH = pl.DeviceIdType.MESH
F32 = jnp.float32
BF16 = jnp.bfloat16
NT = (((1,), (1,)), ((), ()))


def head_norm(values):
    return values * lax.rsqrt(jnp.mean(values * values, axis=-1, keepdims=True) + EPS)


def kernel(
    groups,
    steps,
    step_size,
    step_ids,
    noise_hbm,
    mod_hbm,
    w_in_hbm,
    w_qkv_hbm,
    w_out_hbm,
    w_fin_hbm,
    tk_hbm,
    tv_hbm,
    out_ref,
    noise_raw,
    noise_p,
    mod_v,
    shift_b,
    scale_b,
    gate_b,
    w_in2,
    w_qkv,
    w_out,
    w_fin,
    w_fin2,
    cs_diff,
    tk,
    tv,
    tk_n,
    lat,
    hidden,
    normed,
    att,
    att_par,
    proj,
    mixed,
    u_mine,
    u_send,
    u_recv,
    d_send,
    d_recv,
    load_sem,
    lat_sem,
    att_sem,
    u_sem,
    d_send_sem,
    d_recv_sem,
):
    tok, chan = noise_raw.shape
    width = hidden.shape[1]
    half = width // 2
    own_cols = w_qkv.shape[2]
    pair_cols = 2 * HD
    pairs = own_cols // pair_cols
    txt = tk.shape[0]
    rows = 2 * tok
    pack = tok // 2

    t = lax.axis_index("tm")
    s = lax.axis_index("seq")
    block = lax.rem(t, groups)
    step = t // groups
    partner = (t, 1 - s)

    counter = iter(range(64))

    def load(src, dst):
        copy = pltpu.make_async_copy(src, dst, load_sem.at[next(counter)])
        copy.start()
        return copy

    half_at = pl.multiple_of(s * half, HD)
    ld_noise = load(noise_hbm.at[block], noise_raw)
    ld_in = [load(w_in_hbm, w_in2.at[pl.ds(i * chan, chan)]) for i in range(2)]
    ld_mod = load(mod_hbm, mod_v)
    ld_tk = load(tk_hbm, tk)
    ld_fin = load(w_fin_hbm, w_fin)
    ld_qkv = []
    for p in range(pairs):
        cols = pl.ds(p * pair_cols, pair_cols)
        ld_qkv.append([load(w_qkv_hbm.at[j, :, cols], w_qkv.at[j, :, cols]) for j in range(3)])
        if p == 0:
            ld_tv = load(tv_hbm, tv)
    ld_out = []
    for i in range(2):
        at = pl.multiple_of((s if i == 0 else 1 - s) * own_cols, HD)
        ld_out.append(load(w_out_hbm.at[pl.ds(at, own_cols), pl.ds(half_at, half)], w_out.at[i]))

    barrier = pltpu.get_barrier_semaphore()
    pl.semaphore_signal(barrier, inc=1, device_id=partner, device_id_type=MESH)

    def greet(j, carry):
        @pl.when(j != step)
        def _():
            pl.semaphore_signal(
                barrier, inc=1, device_id=(j * groups + block, s), device_id_type=MESH
            )

        return carry

    lax.fori_loop(0, steps, greet, 0)
    pl.semaphore_wait(barrier, steps)

    lane = lax.broadcasted_iota(jnp.int32, (pack, 2 * chan), 1)
    low = lane < chan

    def put_latent(packed):
        lat[0:pack, :] = jnp.where(low, packed, 0.0).astype(BF16)
        lat[pack:tok, :] = jnp.where(low, 0.0, packed).astype(BF16)

    ld_noise.wait()
    raw = noise_raw[...]
    noise_p[...] = jnp.concatenate([raw[0:pack], raw[pack:tok]], axis=1)
    put_latent(noise_p[...])

    def lat_copy():
        return pltpu.make_async_remote_copy(
            src_ref=lat.at[pl.ds(0, tok)],
            dst_ref=lat.at[pl.ds(tok, tok)],
            send_sem=lat_sem.at[0],
            recv_sem=lat_sem.at[1],
            device_id=partner,
            device_id_type=MESH,
        )

    offsets = sorted(range(1, steps), key=lambda o: abs(o - steps // 2))
    size = step_size[0]

    for sweep in range(ITERS):
        moving = lat_copy()
        moving.start()
        if sweep == 0:
            for c in ld_in:
                c.wait()
        for part in range(2):
            at = pl.ds(part * tok, tok)
            if part == 1:
                moving.wait()
            for c0 in range(0, width, 512):
                cs = pl.ds(c0, 512)
                hidden[at, cs] = jnp.dot(lat[at, :], w_in2[:, cs], preferred_element_type=F32)
            if sweep == 0 and part == 0:
                ld_mod.wait()
                level = step_ids[0]
                ones = jnp.ones((8, 1), F32)
                shift_b[...] = ones * mod_v[0, pl.ds(level, 1), :]
                scale_b[...] = ones * (1.0 + mod_v[1, pl.ds(level, 1), :])
                gate_b[...] = ones * mod_v[2, pl.ds(level, 1), :]
            for r0 in range(part * tok, part * tok + tok, 16):
                rs = pl.ds(r0, 16)
                h = hidden[rs, :]
                mean = jnp.sum(h, axis=-1, keepdims=True) * (1.0 / width)
                c = h - mean
                var = jnp.sum(c * c, axis=-1, keepdims=True) * (1.0 / width)
                n = (c * lax.rsqrt(var + EPS)).reshape(2, 8, width)
                n = n * scale_b[...][None] + shift_b[...][None]
                normed[rs, :] = n.reshape(16, width).astype(BF16)
        if sweep == 0:
            ld_tk.wait()
            for h0 in range(0, own_cols, HD):
                hs = pl.ds(h0, HD)
                tk_n[:, hs] = head_norm(tk[:, hs].astype(F32)).astype(BF16)
            ld_fin.wait()
            fin = w_fin[...]
            w_fin2[0:chan, :] = w_fin[:, pl.ds(half_at, half)]
            w_fin2[chan : 2 * chan, :] = w_fin[:, pl.ds(half_at, half)]
            one = jnp.ones((8, half), BF16)
            cs_own = lax.dot_general(one, w_fin2[...], NT, preferred_element_type=F32)
            cs_all = lax.dot_general(
                jnp.ones((8, width), BF16),
                jnp.concatenate([fin, fin], axis=0),
                NT,
                preferred_element_type=F32,
            )
            cs_diff[...] = 2.0 * cs_own - cs_all

        att_moves = []
        for p in range(pairs):
            cols = pl.ds(p * pair_cols, pair_cols)
            if sweep == 0:
                for c in ld_qkv[p]:
                    c.wait()
                if p == 0:
                    ld_tv.wait()
            q2, k2, v2 = [
                jnp.dot(normed[...], w_qkv[j, :, cols], preferred_element_type=F32)
                for j in range(3)
            ]
            for i in range(2):
                hs = slice(i * HD, (i + 1) * HD)
                at = pl.ds(p * pair_cols + i * HD, HD)
                q = head_norm(q2[:, hs]).astype(BF16)
                k = head_norm(k2[:, hs]).astype(BF16)
                v = v2[:, hs].astype(BF16)
                factor = HD ** (-0.5) * math.log2(math.e)
                own = lax.dot_general(q, k, NT, preferred_element_type=F32)
                far = lax.dot_general(q, tk_n[:, at], NT, preferred_element_type=F32)
                own = jnp.exp2(own * factor)
                far = jnp.exp2(far * factor)
                total = jnp.sum(own, axis=-1, keepdims=True) + jnp.sum(
                    far, axis=-1, keepdims=True
                )
                mix = jnp.dot(own.astype(BF16), v, preferred_element_type=F32)
                mix = mix + jnp.dot(far.astype(BF16), tv[:, at], preferred_element_type=F32)
                att[:, at] = (mix / total).astype(BF16)
            for i in range(2):
                c = pltpu.make_async_remote_copy(
                    src_ref=att.at[pl.ds(i * tok, tok), cols],
                    dst_ref=att_par.at[pl.ds((1 - i) * tok, tok), cols],
                    send_sem=att_sem.at[0, p, i],
                    recv_sem=att_sem.at[1, p, i],
                    device_id=partner,
                    device_id_type=MESH,
                )
                c.start()
                att_moves.append(c)

        if sweep == 0:
            ld_out[0].wait()
        for c0 in range(0, half, 512):
            cs = pl.ds(c0, 512)
            proj[:, cs] = jnp.dot(att[...], w_out[0, :, cs], preferred_element_type=F32)
        if sweep == 0:
            ld_out[1].wait()
        for c in att_moves:
            c.wait()
        for c0 in range(0, half, 512):
            cs = pl.ds(c0, 512)
            from_par = jnp.dot(att_par[...], w_out[1, :, cs], preferred_element_type=F32)
            there = pl.ds(pl.multiple_of(half_at + c0, HD), 512)
            gate = gate_b[0:1, there]
            mixed[:, cs] = hidden[:, there] + gate * (proj[:, cs] + from_par)

        for r0 in range(0, rows, 16):
            rs = pl.ds(r0, 16)
            m = mixed[rs, :]
            mean = jnp.sum(m, axis=-1, keepdims=True) * (1.0 / half)
            c = m - mean
            square = jnp.sum(c * c, axis=-1, keepdims=True)
            u = lax.dot_general(c.astype(BF16), w_fin2[...], NT, preferred_element_type=F32)
            dst = u_mine if r0 < tok else u_send
            ds = pl.ds(r0 % tok, 16)
            dst[0, ds, :] = u
            dst[1, ds, :] = jnp.broadcast_to(mean, (16, 2 * chan))
            dst[2, ds, :] = jnp.broadcast_to(square, (16, 2 * chan))
        c = pltpu.make_async_remote_copy(
            src_ref=u_send,
            dst_ref=u_recv,
            send_sem=u_sem.at[0],
            recv_sem=u_sem.at[1],
            device_id=partner,
            device_id_type=MESH,
        )
        c.start()
        c.wait()
        delta = (u_mine[1] - u_recv[1]) * 0.5
        var = (u_mine[2] + u_recv[2]) * (1.0 / width) + delta * delta
        velocity = u_mine[0] + u_recv[0] + delta * cs_diff[0:1, :]
        velocity = velocity * lax.rsqrt(var + EPS) * size
        drift = jnp.where(low, velocity[0:pack], velocity[pack:tok])
        d_send[sweep] = drift.astype(BF16)

        def send_to(j):
            return pltpu.make_async_remote_copy(
                src_ref=d_send.at[sweep],
                dst_ref=d_recv.at[sweep, step],
                send_sem=d_send_sem.at[sweep],
                recv_sem=d_recv_sem.at[sweep, step],
                device_id=(j * groups + block, s),
                device_id_type=MESH,
            )

        for o in offsets:

            @pl.when(step + o < steps)
            def _():
                send_to(step + o).start()

        def take(j, total):
            pltpu.make_async_remote_copy(
                src_ref=d_send.at[sweep],
                dst_ref=d_recv.at[sweep, j],
                send_sem=d_send_sem.at[sweep],
                recv_sem=d_recv_sem.at[sweep, j],
                device_id=partner,
                device_id_type=MESH,
            ).wait_recv()
            return total + d_recv[sweep, j].astype(F32)

        earlier = lax.fori_loop(0, step, take, jnp.zeros((pack, 2 * chan), F32))
        if sweep < ITERS - 1:
            put_latent(noise_p[...] + earlier)
        else:
            final = noise_p[...] + (earlier + drift)
            out_ref[0:pack, :] = final[:, 0:chan]
            out_ref[pack:tok, :] = final[:, chan : 2 * chan]

        def sent(j, carry):
            send_to(j).wait_send()
            return carry

        lax.fori_loop(step + 1, steps, sent, 0)


def per_device(
    noise, step_size, step_ids, mod_table, w_in, w_qkv, w_out, w_final, text_keys, text_values
):
    groups, tok, chan = noise.shape
    steps = lax.axis_size("tm") // groups
    width = w_in.shape[1]
    half = width // 2
    txt, own_cols = text_keys.shape
    levels = mod_table.shape[0]
    pairs = own_cols // (2 * HD)
    rows = 2 * tok
    pack = tok // 2
    any_spec = pl.BlockSpec(memory_space=pl.ANY)
    smem = pl.BlockSpec(memory_space=pltpu.SMEM)
    vm = pltpu.VMEM
    dma = pltpu.SemaphoreType.DMA
    out = pl.pallas_call(
        functools.partial(kernel, groups, steps),
        out_shape=jax.ShapeDtypeStruct((tok, chan), F32),
        in_specs=[smem, smem] + [any_spec] * 8,
        out_specs=pl.BlockSpec(memory_space=pltpu.VMEM),
        scratch_shapes=[
            vm((tok, chan), F32),
            vm((pack, 2 * chan), F32),
            vm((3, levels, width), F32),
            vm((8, width), F32),
            vm((8, width), F32),
            vm((8, width), F32),
            vm((2 * chan, width), BF16),
            vm((3, width, own_cols), BF16),
            vm((2, own_cols, half), BF16),
            vm((chan, width), BF16),
            vm((2 * chan, half), BF16),
            vm((8, 2 * chan), F32),
            vm((txt, own_cols), BF16),
            vm((txt, own_cols), BF16),
            vm((txt, own_cols), BF16),
            vm((rows, 2 * chan), BF16),
            vm((rows, width), F32),
            vm((rows, width), BF16),
            vm((rows, own_cols), BF16),
            vm((rows, own_cols), BF16),
            vm((rows, half), F32),
            vm((rows, half), F32),
            vm((3, tok, 2 * chan), F32),
            vm((3, tok, 2 * chan), F32),
            vm((3, tok, 2 * chan), F32),
            vm((ITERS, pack, 2 * chan), BF16),
            vm((ITERS, steps, pack, 2 * chan), BF16),
            dma((24,)),
            dma((2,)),
            dma((2, pairs, 2)),
            dma((2,)),
            dma((ITERS,)),
            dma((ITERS, steps)),
        ],
        compiler_params=pltpu.CompilerParams(
            collective_id=0, has_side_effects=True, vmem_limit_bytes=56 * 2**20
        ),
        cost_estimate=pl.CostEstimate(
            flops=5 * 10**9, bytes_accessed=25 * 10**6, transcendentals=10**6
        ),
        name="picard",
    )(
        step_size,
        step_ids,
        noise,
        jnp.transpose(mod_table, (1, 0, 2)),
        w_in,
        jnp.transpose(w_qkv, (1, 0, 2)),
        w_out,
        jnp.transpose(w_final, (1, 0)),
        text_keys,
        text_values,
    )
    return out[None]


def solution(mesh):
    placed = (
        P(None, "seq", None),
        P("tm"),
        P("tm"),
        P(),
        P(),
        P(None, None, "seq"),
        P(),
        P(),
        P(None, "seq"),
        P(None, "seq"),
    )
    return jax.shard_map(
        per_device, mesh=mesh, in_specs=placed, out_specs=P("tm", "seq", None), check_vma=False
    )
```

time: 677 us -> 42.2 us (0.06); the launches traced: 666 us -> 41.8 us
  waiting for transfers between devices: 331 us -> 0 us
  other arithmetic: 248 us -> 0 us
  Pallas kernels: 0 us -> 39.1 us
  local copies, waits for them, and re-layouts: 31.7 us -> 1.38 us
  matrix products: 29.8 us -> 0 us
  between operations: 14.9 us -> 1.3 us
    all_gather x2 -> x0, waiting for transfers between devices: 302 us -> none  [carried_in(): pieces = lax.all_gather(value, axis)]
    select_n x254 -> x0, other arithmetic: 241 us -> none  [lap(): return jnp.where(position < mine, longer, total)]
    pallas_call x0 -> x1, Pallas kernels: none -> 39.1 us  [per_device(): pl.pallas_call(functools.partial(kernel, groups, steps), out_shape=jax.Sh...]
    dot_general x17 -> x0, matrix products: 29.8 us -> none  [the longest x2 14.3 us: per_device(): jnp.einsum('tsd,de->tse', lax.all_gather(normed, 'seq', axis=0, tiled=Tru...]
    reduce_scatter x2 -> x0, waiting for transfers between devices: 28.1 us -> none  [per_device(): lax.psum_scatter(jnp.einsum('tsh,hd->tsd', attended, my_rows, preferred_e...]
    unnamed x32 -> x1, local copies, waits for them, and re-layouts: 27.6 us -> 1.38 us
  transfers between devices with their start and end apart: 4 -> 0, of which waited for: 4 -> 0; matrix products, arithmetic and copies ran while one was open for 0% -> 0% of each run, Pallas kernels for 0% -> 0%
where the time goes in v1:
time: 42.2 us; the launch traced here: 41.8 us
  Pallas kernels  39.1 us (93%)
  local copies, waits for them, and re-layouts  1.38 us (3%)
  between operations  1.3 us (3%)
    pallas_call x1, Pallas kernels, per_device(): pl.pallas_call(functools.partial(kernel, groups, steps), out_shape=jax.Sh...  39.1 us
    unnamed x1, local copies, waits for them, and re-layouts  1.38 us

profile of v1, /device:TPU:226, one launch (start us, length us, event | category | flops | bytes accessed | tf_op | source)
XLA Modules:
  0.0 41.8 jit_solution(9633920990951141110)
XLA Ops:
  1.3 39.1 %picard.1 = f32[64,64]{1,0:T(8,128)} custom-call(f32[1]{0:T(128)S(6)} %copy.12.step_size, s32[1]{0:T(128)S(6)} %copy.13.step_ids, f32[8,64,64]{2,1,0:T(8,128)} %noise_hbm.1, f32[3,50,3072]{2,1,0:T(8,128)} %bitcast.5, bf16[64,3072]{1,0:T(8,128)(2,1)} %w_in_hbm.1, bf16[3,3072,768]{2,1,0:T(8,128)(2,1)} %bitcast.4, bf16[1536,3072]{1,0:T(8,128)(2,1)} %w_out_hbm.1, ...), custom_call_target="tpu_custom_call" | custom-call | flops 5000000000 | bytes 25000000 | tf_op jit(solution)/shard_map/picard/pallas_call | solution.py:344
  40.4 1.4 %copy.14 = f32[1,64,64]{2,1,0:T(8,128)} copy(f32[1,64,64]{2,1,0:T(8,128)} %bitcast.7) | data formatting | bytes 32768

commit v2 on v1

v2 whole, which is shorter than its diff:
```python
import functools
import math

import jax
import jax.numpy as jnp
from jax import lax
from jax.experimental import pallas as pl
from jax.experimental.pallas import tpu as pltpu
from jax.sharding import PartitionSpec as P

HD = 128
ITERS = 2
EPS = 1e-06
MESH = pl.DeviceIdType.MESH
F32 = jnp.float32
BF16 = jnp.bfloat16
NT = (((1,), (1,)), ((), ()))


def head_norm(values):
    return values * lax.rsqrt(jnp.mean(values * values, axis=-1, keepdims=True) + EPS)


def kernel(
    groups,
    steps,
    step_size_hbm,
    step_ids_hbm,
    noise_hbm,
    mod_hbm,
    w_in_hbm,
    w_qkv_hbm,
    w_out_hbm,
    w_fin_hbm,
    tk_hbm,
    tv_hbm,
    out_ref,
    size_s,
    level_s,
    noise_raw,
    noise_p,
    mod_v,
    gate_v,
    shift_b,
    scale_b,
    gate_b,
    w_in2,
    w_qkv,
    w_out,
    w_fin,
    w_fin_t,
    cs_diff,
    tk,
    tv,
    tk_t,
    lat,
    hidden,
    normed,
    q_s,
    k_s,
    v_s,
    q_n,
    k_n,
    p_s,
    l_s,
    att,
    att_par,
    proj,
    mixed,
    centred,
    u_mine,
    u_send,
    u_recv,
    d_send,
    d_recv,
    load_sem,
    lat_sem,
    att_sem,
    u_sem,
    d_send_sem,
    d_recv_sem,
):
    tok, chan = noise_raw.shape
    width = hidden.shape[1]
    half = width // 2
    own_cols = w_qkv.shape[2]
    heads = own_cols // HD
    pair_cols = 2 * HD
    pairs = own_cols // pair_cols
    txt = tk.shape[0]
    rows = 2 * tok
    keys = rows + txt
    pack = tok // 2

    t = lax.axis_index("tm")
    s = lax.axis_index("seq")
    block = lax.rem(t, groups)
    step = t // groups
    partner = (t, 1 - s)

    counter = iter(range(64))

    def load(src, dst):
        copy = pltpu.make_async_copy(src, dst, load_sem.at[next(counter)])
        copy.start()
        return copy

    half_at = pl.multiple_of(s * half, HD)
    ld_noise = load(noise_hbm.at[block], noise_raw)
    ld_ids = load(step_ids_hbm, level_s)
    ld_size = load(step_size_hbm, size_s)
    ld_in = load(w_in_hbm, w_in2.at[pl.ds(0, chan)])
    ld_mod = load(mod_hbm.at[pl.ds(0, 2)], mod_v)
    ld_tk = load(tk_hbm, tk)
    ld_qkv = []
    for j in range(3):
        if j == 2:
            ld_tv = load(tv_hbm, tv)
            ld_fin = load(w_fin_hbm, w_fin)
        for p in range(pairs):
            cols = pl.ds(p * pair_cols, pair_cols)
            ld_qkv.append(load(w_qkv_hbm.at[j, :, cols], w_qkv.at[j, :, cols]))
    ld_out = []
    for i in range(2):
        at = pl.multiple_of((s if i == 0 else 1 - s) * own_cols, HD)
        ld_out.append(load(w_out_hbm.at[pl.ds(at, own_cols), pl.ds(half_at, half)], w_out.at[i]))
        if i == 0:
            ld_gate = load(mod_hbm.at[2], gate_v)

    barrier = pltpu.get_barrier_semaphore()

    @pl.when(s == 0)
    def _():
        pl.semaphore_signal(barrier, inc=1, device_id=partner, device_id_type=MESH)

    lane = lax.broadcasted_iota(jnp.int32, (pack, 2 * chan), 1)
    low = lane < chan

    def put_latent(packed):
        lat[0:pack, :] = jnp.where(low, packed, 0.0).astype(BF16)
        lat[pack:tok, :] = jnp.where(low, 0.0, packed).astype(BF16)

    ld_noise.wait()
    raw = noise_raw[...]
    noise_p[...] = jnp.concatenate([raw[0:pack], raw[pack:tok]], axis=1)
    put_latent(noise_p[...])

    lat_move = pltpu.make_async_remote_copy(
        src_ref=lat.at[pl.ds(0, tok)],
        dst_ref=lat.at[pl.ds(tok, tok)],
        send_sem=lat_sem.at[0],
        recv_sem=lat_sem.at[1],
        device_id=partner,
        device_id_type=MESH,
    )

    def att_move(p, i):
        cols = pl.ds(p * pair_cols, pair_cols)
        return pltpu.make_async_remote_copy(
            src_ref=att.at[pl.ds(i * tok, tok), cols],
            dst_ref=att_par.at[pl.ds((1 - i) * tok, tok), cols],
            send_sem=att_sem.at[0, p, i],
            recv_sem=att_sem.at[1, p, i],
            device_id=partner,
            device_id_type=MESH,
        )

    u_move = pltpu.make_async_remote_copy(
        src_ref=u_send,
        dst_ref=u_recv,
        send_sem=u_sem.at[0],
        recv_sem=u_sem.at[1],
        device_id=partner,
        device_id_type=MESH,
    )

    def embed(part):
        at = pl.ds(part * tok, tok)
        for c0 in range(0, width, 512):
            cs = pl.ds(c0, 512)
            hidden[at, cs] = jnp.dot(lat[at, :], w_in2[:, cs], preferred_element_type=F32)

    def modulate(part):
        for r0 in range(part * tok, part * tok + tok, 16):
            rs = pl.ds(r0, 16)
            total = jnp.zeros((16, HD), F32)
            for c0 in range(0, width, HD):
                total = total + hidden[rs, pl.ds(c0, HD)]
            mean = jnp.sum(total, axis=-1, keepdims=True) * (1.0 / width)
            mean = jnp.broadcast_to(mean, (16, HD))
            total = jnp.zeros((16, HD), F32)
            for c0 in range(0, width, HD):
                c = hidden[rs, pl.ds(c0, HD)] - mean
                total = total + c * c
            var = jnp.sum(total, axis=-1, keepdims=True) * (1.0 / width)
            rstd = jnp.broadcast_to(lax.rsqrt(var + EPS), (16, HD))
            for c0 in range(0, width, HD):
                cs = pl.ds(c0, HD)
                n = (hidden[rs, cs] - mean) * rstd
                scale = jnp.concatenate([scale_b[:, cs]] * 2, axis=0)
                shift = jnp.concatenate([shift_b[:, cs]] * 2, axis=0)
                normed[rs, cs] = (n * scale + shift).astype(BF16)

    def project(j, p):
        cols = pl.ds(p * pair_cols, pair_cols)
        dst = (q_s, k_s, v_s)[j]
        dst[:, cols] = jnp.dot(
            normed[...], w_qkv[j, :, cols], preferred_element_type=F32
        ).astype(dst.dtype)

    def norm_heads(src, dst):
        for h in range(heads):
            at = pl.ds(h * HD, HD)
            dst[:, at] = head_norm(src[:, at]).astype(BF16)

    factor = HD ** (-0.5) * math.log2(math.e)

    def score(h):
        at = pl.ds(h * HD, HD)
        q = q_n[:, at]
        own = lax.dot_general(q, k_n[:, at], NT, preferred_element_type=F32)
        far = jnp.dot(q, tk_t[at, :], preferred_element_type=F32)
        own = jnp.exp2(own * factor)
        far = jnp.exp2(far * factor)
        p_s[h, :, 0:rows] = own.astype(BF16)
        p_s[h, :, rows:keys] = far.astype(BF16)
        total = jnp.sum(own, axis=-1, keepdims=True) + jnp.sum(far, axis=-1, keepdims=True)
        l_s[h] = jnp.broadcast_to(total, (rows, HD))

    def weigh(h):
        at = pl.ds(h * HD, HD)
        mix = jnp.dot(p_s[h, :, 0:rows], v_s[:, at], preferred_element_type=F32)
        mix = mix + jnp.dot(p_s[h, :, rows:keys], tv[:, at], preferred_element_type=F32)
        att[:, at] = (mix / l_s[h]).astype(BF16)

    offsets = sorted(range(1, steps), key=lambda o: abs(o - steps // 2))

    for sweep in range(ITERS):
        first = sweep == 0
        if first:

            @pl.when(s == 1)
            def _():
                pl.semaphore_wait(barrier, 1)
                lat_move.start()

            ld_in.wait()
            w_in2[chan : 2 * chan, :] = w_in2[0:chan, :]
        else:
            lat_move.start()
        embed(0)
        if first:
            ld_ids.wait()
            ld_mod.wait()
            level = level_s[0]
            ones = jnp.ones((8, 1), F32)
            shift_b[...] = ones * mod_v[0, pl.ds(level, 1), :]
            scale_b[...] = ones * (1.0 + mod_v[1, pl.ds(level, 1), :])
        modulate(0)
        lat_move.wait_recv()
        if first:

            @pl.when(s == 0)
            def _():
                lat_move.start()

                def greet(j, carry):
                    @pl.when(j != step)
                    def _():
                        pl.semaphore_signal(
                            barrier, inc=1, device_id=(j * groups + block, 0), device_id_type=MESH
                        )

                    return carry

                lax.fori_loop(0, steps, greet, 0)

        embed(1)
        modulate(1)
        lat_move.wait_send()
        if first:
            ld_tk.wait()
            for h0 in range(0, own_cols, HD):
                hs = pl.ds(h0, HD)
                tk_t[hs, :] = jnp.transpose(head_norm(tk[:, hs].astype(F32))).astype(BF16)

        for j in range(3):
            if first and j == 2:
                ld_tv.wait()
                ld_fin.wait()
                one = jnp.ones((8, width), BF16)
                both = jnp.concatenate([w_fin[...]] * 2, axis=0)
                cs_all = lax.dot_general(one, both, NT, preferred_element_type=F32)
                for c0 in range(0, half, HD):
                    piece = w_fin[:, pl.ds(pl.multiple_of(half_at + c0, HD), HD)].astype(F32)
                    piece = jnp.concatenate([piece, piece], axis=0)
                    w_fin_t[pl.ds(c0, HD), :] = jnp.transpose(piece).astype(BF16)
                cs_own = jnp.dot(one[:, 0:half], w_fin_t[...], preferred_element_type=F32)
                cs_diff[...] = 2.0 * cs_own - cs_all
            for p in range(pairs):
                if first:
                    ld_qkv[j * pairs + p].wait()
                project(j, p)
                if j == 2:
                    for h in (2 * p, 2 * p + 1):
                        weigh(h)
                    for i in range(2):
                        att_move(p, i).start()
            if j == 0:
                norm_heads(q_s, q_n)
            if j == 1:
                norm_heads(k_s, k_n)
                for h in range(heads):
                    score(h)

        if first:
            ld_out[0].wait()
        for c0 in range(0, half, 512):
            cs = pl.ds(c0, 512)
            proj[:, cs] = jnp.dot(att[...], w_out[0, :, cs], preferred_element_type=F32)
        if first:
            ld_out[1].wait()
            ld_gate.wait()
            gate_b[...] = ones * gate_v[pl.ds(level, 1), :]
        for p in range(pairs):
            for i in range(2):
                att_move(p, i).wait()
        for c0 in range(0, half, 512):
            cs = pl.ds(c0, 512)
            from_par = jnp.dot(att_par[...], w_out[1, :, cs], preferred_element_type=F32)
            there = pl.ds(pl.multiple_of(half_at + c0, HD), 512)
            gate = gate_b[0:1, there]
            mixed[:, cs] = hidden[:, there] + gate * (proj[:, cs] + from_par)

        for r0 in range(0, rows, 16):
            rs = pl.ds(r0, 16)
            m = mixed[rs, :]
            mean = jnp.sum(m, axis=-1, keepdims=True) * (1.0 / half)
            c = m - mean
            square = jnp.sum(c * c, axis=-1, keepdims=True)
            centred[rs, :] = c.astype(BF16)
            dst = u_mine if r0 < tok else u_send
            ds = pl.ds(r0 % tok, 16)
            dst[1, ds, :] = jnp.broadcast_to(mean, (16, 2 * chan))
            dst[2, ds, :] = jnp.broadcast_to(square, (16, 2 * chan))
        u = jnp.dot(centred[...], w_fin_t[...], preferred_element_type=F32)
        u_mine[0] = u[0:tok]
        u_send[0] = u[tok:rows]
        if first:

            @pl.when(s == 0)
            def _():
                pl.semaphore_wait(barrier, steps - 1)

            ld_size.wait()
        u_move.start()
        u_move.wait()
        delta = (u_mine[1] - u_recv[1]) * 0.5
        var = (u_mine[2] + u_recv[2]) * (1.0 / width) + delta * delta
        velocity = u_mine[0] + u_recv[0] + delta * cs_diff[0:1, :]
        velocity = velocity * lax.rsqrt(var + EPS) * size_s[0]
        drift = jnp.where(low, velocity[0:pack], velocity[pack:tok])
        d_send[sweep] = drift.astype(BF16)

        def send_to(j):
            return pltpu.make_async_remote_copy(
                src_ref=d_send.at[sweep],
                dst_ref=d_recv.at[sweep, step],
                send_sem=d_send_sem.at[sweep],
                recv_sem=d_recv_sem.at[sweep, step],
                device_id=(j * groups + block, s),
                device_id_type=MESH,
            )

        for o in offsets:

            @pl.when(step + o < steps)
            def _():
                send_to(step + o).start()

        def take(j, total):
            pltpu.make_async_remote_copy(
                src_ref=d_send.at[sweep],
                dst_ref=d_recv.at[sweep, j],
                send_sem=d_send_sem.at[sweep],
                recv_sem=d_recv_sem.at[sweep, j],
                device_id=partner,
                device_id_type=MESH,
            ).wait_recv()
            return total + d_recv[sweep, j].astype(F32)

        earlier = lax.fori_loop(0, step, take, jnp.zeros((pack, 2 * chan), F32))
        if sweep < ITERS - 1:
            put_latent(noise_p[...] + earlier)
        else:
            final = noise_p[...] + (earlier + drift)
            out_ref[0:pack, :] = final[:, 0:chan]
            out_ref[pack:tok, :] = final[:, chan : 2 * chan]

        def sent(j, carry):
            send_to(j).wait_send()
            return carry

        lax.fori_loop(step + 1, steps, sent, 0)


def per_device(
    noise, step_size, step_ids, mod_table, w_in, w_qkv, w_out, w_final, text_keys, text_values
):
    groups, tok, chan = noise.shape
    steps = lax.axis_size("tm") // groups
    width = w_in.shape[1]
    half = width // 2
    txt, own_cols = text_keys.shape
    levels = mod_table.shape[0]
    heads = own_cols // HD
    pairs = heads // 2
    rows = 2 * tok
    pack = tok // 2
    any_spec = pl.BlockSpec(memory_space=pl.ANY)
    vm = pltpu.VMEM
    dma = pltpu.SemaphoreType.DMA
    out = pl.pallas_call(
        functools.partial(kernel, groups, steps),
        out_shape=jax.ShapeDtypeStruct((tok, chan), F32),
        in_specs=[any_spec] * 10,
        out_specs=pl.BlockSpec(memory_space=pltpu.VMEM),
        scratch_shapes=[
            pltpu.SMEM((1,), F32),
            pltpu.SMEM((1,), jnp.int32),
            vm((tok, chan), F32),
            vm((pack, 2 * chan), F32),
            vm((2, levels, width), F32),
            vm((levels, width), F32),
            vm((8, width), F32),
            vm((8, width), F32),
            vm((8, width), F32),
            vm((2 * chan, width), BF16),
            vm((3, width, own_cols), BF16),
            vm((2, own_cols, half), BF16),
            vm((chan, width), BF16),
            vm((half, 2 * chan), BF16),
            vm((8, 2 * chan), F32),
            vm((txt, own_cols), BF16),
            vm((txt, own_cols), BF16),
            vm((own_cols, txt), BF16),
            vm((rows, 2 * chan), BF16),
            vm((rows, width), F32),
            vm((rows, width), BF16),
            vm((rows, own_cols), F32),
            vm((rows, own_cols), F32),
            vm((rows, own_cols), BF16),
            vm((rows, own_cols), BF16),
            vm((rows, own_cols), BF16),
            vm((heads, rows, rows + txt), BF16),
            vm((heads, rows, HD), F32),
            vm((rows, own_cols), BF16),
            vm((rows, own_cols), BF16),
            vm((rows, half), F32),
            vm((rows, half), F32),
            vm((rows, half), BF16),
            vm((3, tok, 2 * chan), F32),
            vm((3, tok, 2 * chan), F32),
            vm((3, tok, 2 * chan), F32),
            vm((ITERS, pack, 2 * chan), BF16),
            vm((ITERS, steps, pack, 2 * chan), BF16),
            dma((24,)),
            dma((2,)),
            dma((2, pairs, 2)),
            dma((2,)),
            dma((ITERS,)),
            dma((ITERS, steps)),
        ],
        compiler_params=pltpu.CompilerParams(
            collective_id=0, has_side_effects=True, vmem_limit_bytes=56 * 2**20
        ),
        cost_estimate=pl.CostEstimate(
            flops=5 * 10**9, bytes_accessed=25 * 10**6, transcendentals=10**6
        ),
        name="picard",
    )(
        step_size,
        step_ids,
        noise,
        jnp.transpose(mod_table, (1, 0, 2)),
        w_in,
        jnp.transpose(w_qkv, (1, 0, 2)),
        w_out,
        jnp.transpose(w_final, (1, 0)),
        text_keys,
        text_values,
    )
    return out[None]


def solution(mesh):
    placed = (
        P(None, "seq", None),
        P("tm"),
        P("tm"),
        P(),
        P(),
        P(None, None, "seq"),
        P(),
        P(),
        P(None, "seq"),
        P(None, "seq"),
    )
    return jax.shard_map(
        per_device, mesh=mesh, in_specs=placed, out_specs=P("tm", "seq", None), check_vma=False
    )
```

time: 42.2 us -> 36.5 us (0.86)
  Pallas kernels: 39.1 us -> 33.6 us
    pallas_call x1, Pallas kernels: 39.1 us -> 33.6 us  [per_device(): pl.pallas_call(functools.partial(kernel, groups, steps), out_shape=jax.Sh...]
where the time goes in v2:
time: 36.5 us; the launch traced here: 36.3 us
  Pallas kernels  33.6 us (92%)
  local copies, waits for them, and re-layouts  1.38 us (4%)
  between operations  1.3 us (4%)
    pallas_call x1, Pallas kernels, per_device(): pl.pallas_call(functools.partial(kernel, groups, steps), out_shape=jax.Sh...  33.6 us
    unnamed x1, local copies, waits for them, and re-layouts  1.38 us

profile of v2, /device:TPU:226, one launch (start us, length us, event | category | flops | bytes accessed | tf_op | source)
XLA Modules:
  0.0 36.3 jit_solution(2286440806713813417)
XLA Ops:
  1.3 33.6 %picard.1 = f32[64,64]{1,0:T(8,128)} custom-call(f32[1]{0:T(128)S(6)} %copy.12.step_size_hbm, s32[1]{0:T(128)S(6)} %copy.13.step_ids_hbm, f32[8,64,64]{2,1,0:T(8,128)} %noise_hbm.1, f32[3,50,3072]{2,1,0:T(8,128)} %bitcast.5, bf16[64,3072]{1,0:T(8,128)(2,1)} %w_in_hbm.1, bf16[3,3072,768]{2,1,0:T(8,128)(2,1)} %bitcast.4, bf16[1536,3072]{1,0:T(8,128)(2,1)} %w_out_hbm.1, ...), custom_call_target="tpu_custom_call" | custom-call | flops 5000000000 | bytes 25000000 | tf_op jit(solution)/shard_map/picard/pallas_call | solution.py:423
  35.0 1.4 %copy.14 = f32[1,64,64]{2,1,0:T(8,128)} copy(f32[1,64,64]{2,1,0:T(8,128)} %bitcast.7) | data formatting | bytes 32768

commit v3 on v2

--- a/solution.py
+++ b/solution.py
@@ -74,6 +74,7 @@
     d_send,
     d_recv,
     load_sem,
+    in_sem,
     lat_sem,
     att_sem,
     u_sem,
@@ -98,6 +99,12 @@
     step = t // groups
     partner = (t, 1 - s)
 
+    barrier = pltpu.get_barrier_semaphore()
+
+    @pl.when(s == 0)
+    def _():
+        pl.semaphore_signal(barrier, inc=1, device_id=partner, device_id_type=MESH)
+
     counter = iter(range(64))
 
     def load(src, dst):
@@ -114,9 +121,10 @@
     ld_tk = load(tk_hbm, tk)
     ld_qkv = []
     for j in range(3):
+        if j == 1:
+            ld_fin = load(w_fin_hbm, w_fin)
         if j == 2:
             ld_tv = load(tv_hbm, tv)
-            ld_fin = load(w_fin_hbm, w_fin)
         for p in range(pairs):
             cols = pl.ds(p * pair_cols, pair_cols)
             ld_qkv.append(load(w_qkv_hbm.at[j, :, cols], w_qkv.at[j, :, cols]))
@@ -127,11 +135,25 @@
         if i == 0:
             ld_gate = load(mod_hbm.at[2], gate_v)
 
-    barrier = pltpu.get_barrier_semaphore()
+    @pl.when(s == 1)
+    def _():
+        pl.semaphore_wait(barrier, 1)
+        pl.semaphore_signal(in_sem, inc=1, device_id=partner, device_id_type=MESH)
 
     @pl.when(s == 0)
     def _():
-        pl.semaphore_signal(barrier, inc=1, device_id=partner, device_id_type=MESH)
+        pl.semaphore_wait(in_sem, 1)
+
+        def greet(j, carry):
+            @pl.when(j != step)
+            def _():
+                pl.semaphore_signal(
+                    barrier, inc=1, device_id=(j * groups + block, 0), device_id_type=MESH
+                )
+
+            return carry
+
+        lax.fori_loop(0, steps, greet, 0)
 
     lane = lax.broadcasted_iota(jnp.int32, (pack, 2 * chan), 1)
     low = lane < chan
@@ -233,21 +255,31 @@
         mix = mix + jnp.dot(p_s[h, :, rows:keys], tv[:, at], preferred_element_type=F32)
         att[:, at] = (mix / l_s[h]).astype(BF16)
 
+    def text_head(h):
+        at = pl.ds(h * HD, HD)
+        tk_t[at, :] = jnp.transpose(head_norm(tk[:, at].astype(F32)).astype(BF16))
+
+    def final_weights():
+        mine = jnp.zeros((chan, HD), F32)
+        other = jnp.zeros((chan, HD), F32)
+        for c0 in range(0, half, HD):
+            piece = w_fin[:, pl.ds(pl.multiple_of(half_at + c0, HD), HD)]
+            w_fin_t[pl.ds(c0, HD), :] = jnp.transpose(jnp.concatenate([piece, piece], axis=0))
+            mine = mine + piece.astype(F32)
+            piece = w_fin[:, pl.ds(pl.multiple_of(half - half_at + c0, HD), HD)]
+            other = other + piece.astype(F32)
+        total = jnp.sum(mine - other, axis=-1, keepdims=True)
+        total = jnp.broadcast_to(total, (chan, HD))
+        cs_diff[...] = jnp.transpose(jnp.concatenate([total, total], axis=0))[0:8]
+
     offsets = sorted(range(1, steps), key=lambda o: abs(o - steps // 2))
 
     for sweep in range(ITERS):
         first = sweep == 0
+        lat_move.start()
         if first:
-
-            @pl.when(s == 1)
-            def _():
-                pl.semaphore_wait(barrier, 1)
-                lat_move.start()
-
             ld_in.wait()
             w_in2[chan : 2 * chan, :] = w_in2[0:chan, :]
-        else:
-            lat_move.start()
         embed(0)
         if first:
             ld_ids.wait()
@@ -258,60 +290,44 @@
             scale_b[...] = ones * (1.0 + mod_v[1, pl.ds(level, 1), :])
         modulate(0)
         lat_move.wait_recv()
-        if first:
-
-            @pl.when(s == 0)
-            def _():
-                lat_move.start()
-
-                def greet(j, carry):
-                    @pl.when(j != step)
-                    def _():
-                        pl.semaphore_signal(
-                            barrier, inc=1, device_id=(j * groups + block, 0), device_id_type=MESH
-                        )
-
-                    return carry
-
-                lax.fori_loop(0, steps, greet, 0)
-
         embed(1)
         modulate(1)
         lat_move.wait_send()
         if first:
-            ld_tk.wait()
-            for h0 in range(0, own_cols, HD):
-                hs = pl.ds(h0, HD)
-                tk_t[hs, :] = jnp.transpose(head_norm(tk[:, hs].astype(F32))).astype(BF16)
-
-        for j in range(3):
-            if first and j == 2:
-                ld_tv.wait()
-                ld_fin.wait()
-                one = jnp.ones((8, width), BF16)
-                both = jnp.concatenate([w_fin[...]] * 2, axis=0)
-                cs_all = lax.dot_general(one, both, NT, preferred_element_type=F32)
-                for c0 in range(0, half, HD):
-                    piece = w_fin[:, pl.ds(pl.multiple_of(half_at + c0, HD), HD)].astype(F32)
-                    piece = jnp.concatenate([piece, piece], axis=0)
-                    w_fin_t[pl.ds(c0, HD), :] = jnp.transpose(piece).astype(BF16)
-                cs_own = jnp.dot(one[:, 0:half], w_fin_t[...], preferred_element_type=F32)
-                cs_diff[...] = 2.0 * cs_own - cs_all
             for p in range(pairs):
-                if first:
-                    ld_qkv[j * pairs + p].wait()
-                project(j, p)
-                if j == 2:
-                    for h in (2 * p, 2 * p + 1):
-                        weigh(h)
-                    for i in range(2):
-                        att_move(p, i).start()
-            if j == 0:
-                norm_heads(q_s, q_n)
-            if j == 1:
-                norm_heads(k_s, k_n)
-                for h in range(heads):
-                    score(h)
+                ld_qkv[p].wait()
+                project(0, p)
+                if p == 0:
+                    ld_tk.wait()
+                for h in (2 * p, 2 * p + 1):
+                    text_head(h)
+            norm_heads(q_s, q_n)
+            for p in range(pairs):
+                ld_qkv[pairs + p].wait()
+                project(1, p)
+                if p == 0:
+                    ld_fin.wait()
+                    final_weights()
+            norm_heads(k_s, k_n)
+            for h in range(heads):
+                score(h)
+            for p in range(pairs):
+                ld_qkv[2 * pairs + p].wait()
+                project(2, p)
+            ld_tv.wait()
+        else:
+            for j in range(3):
+                for p in range(pairs):
+                    project(j, p)
+            norm_heads(q_s, q_n)
+            norm_heads(k_s, k_n)
+            for h in range(heads):
+                score(h)
+        for p in range(pairs):
+            for h in (2 * p, 2 * p + 1):
+                weigh(h)
+            for i in range(2):
+                att_move(p, i).start()
 
         if first:
             ld_out[0].wait()
@@ -397,11 +413,19 @@
             out_ref[0:pack, :] = final[:, 0:chan]
             out_ref[pack:tok, :] = final[:, chan : 2 * chan]
 
-        def sent(j, carry):
-            send_to(j).wait_send()
-            return carry
-
-        lax.fori_loop(step + 1, steps, sent, 0)
+    def sent(j, carry):
+        for sweep in range(ITERS):
+            pltpu.make_async_remote_copy(
+                src_ref=d_send.at[sweep],
+                dst_ref=d_recv.at[sweep, step],
+                send_sem=d_send_sem.at[sweep],
+                recv_sem=d_recv_sem.at[sweep, step],
+                device_id=partner,
+                device_id_type=MESH,
+            ).wait_send()
+        return carry
+
+    lax.fori_loop(step + 1, steps, sent, 0)
 
 
 def per_device(
@@ -417,13 +441,13 @@
     pairs = heads // 2
     rows = 2 * tok
     pack = tok // 2
-    any_spec = pl.BlockSpec(memory_space=pl.ANY)
+    hbm = pl.BlockSpec(memory_space=pltpu.HBM)
     vm = pltpu.VMEM
     dma = pltpu.SemaphoreType.DMA
     out = pl.pallas_call(
         functools.partial(kernel, groups, steps),
         out_shape=jax.ShapeDtypeStruct((tok, chan), F32),
-        in_specs=[any_spec] * 10,
+        in_specs=[hbm] * 10,
         out_specs=pl.BlockSpec(memory_space=pltpu.VMEM),
         scratch_shapes=[
             pltpu.SMEM((1,), F32),
@@ -465,6 +489,7 @@
             vm((ITERS, pack, 2 * chan), BF16),
             vm((ITERS, steps, pack, 2 * chan), BF16),
             dma((24,)),
+            pltpu.SemaphoreType.REGULAR,
             dma((2,)),
             dma((2, pairs, 2)),
             dma((2,)),

time: 36.5 us -> 33.7 us (0.923)
  Pallas kernels: 33.6 us -> 30.8 us
    pallas_call x1, Pallas kernels: 33.6 us -> 30.8 us  [per_device(): pl.pallas_call(functools.partial(kernel, groups, steps), out_shape=jax.Sh...]
where the time goes in v3:
time: 33.7 us; the launch traced here: 33.5 us
  Pallas kernels  30.8 us (91%)
  local copies, waits for them, and re-layouts  1.38 us (4%)
  between operations  1.3 us (4%)
    pallas_call x1, Pallas kernels, per_device(): pl.pallas_call(functools.partial(kernel, groups, steps), out_shape=jax.Sh...  30.8 us
    unnamed x1, local copies, waits for them, and re-layouts  1.38 us

profile of v3, /device:TPU:226, one launch (start us, length us, event | category | flops | bytes accessed | tf_op | source)
XLA Modules:
  0.0 33.5 jit_solution(2615459188688033058)
XLA Ops:
  1.3 30.8 %picard.1 = f32[64,64]{1,0:T(8,128)} custom-call(f32[1]{0:T(128)S(6)} %copy.12.step_size_hbm, s32[1]{0:T(128)S(6)} %copy.13.step_ids_hbm, f32[8,64,64]{2,1,0:T(8,128)} %noise_hbm.1, f32[3,50,3072]{2,1,0:T(8,128)} %bitcast.5, bf16[64,3072]{1,0:T(8,128)(2,1)} %w_in_hbm.1, bf16[3,3072,768]{2,1,0:T(8,128)(2,1)} %bitcast.4, bf16[1536,3072]{1,0:T(8,128)(2,1)} %w_out_hbm.1, ...), custom_call_target="tpu_custom_call" | custom-call | flops 5000000000 | bytes 25000000 | tf_op jit(solution)/shard_map/picard/pallas_call | solution.py:447
  32.1 1.4 %copy.14 = f32[1,64,64]{2,1,0:T(8,128)} copy(f32[1,64,64]{2,1,0:T(8,128)} %bitcast.7) | data formatting | bytes 32768

commit v4 on v3

--- a/solution.py
+++ b/solution.py
@@ -125,15 +125,18 @@
             ld_fin = load(w_fin_hbm, w_fin)
         if j == 2:
             ld_tv = load(tv_hbm, tv)
+            ld_gate = load(mod_hbm.at[2], gate_v)
         for p in range(pairs):
             cols = pl.ds(p * pair_cols, pair_cols)
             ld_qkv.append(load(w_qkv_hbm.at[j, :, cols], w_qkv.at[j, :, cols]))
     ld_out = []
-    for i in range(2):
-        at = pl.multiple_of((s if i == 0 else 1 - s) * own_cols, HD)
-        ld_out.append(load(w_out_hbm.at[pl.ds(at, own_cols), pl.ds(half_at, half)], w_out.at[i]))
-        if i == 0:
-            ld_gate = load(mod_hbm.at[2], gate_v)
+
+    def load_out():
+        for i in range(2):
+            at = pl.multiple_of((s if i == 0 else 1 - s) * own_cols, HD)
+            ld_out.append(
+                load(w_out_hbm.at[pl.ds(at, own_cols), pl.ds(half_at, half)], w_out.at[i])
+            )
 
     @pl.when(s == 1)
     def _():
@@ -293,36 +296,29 @@
         embed(1)
         modulate(1)
         lat_move.wait_send()
+        for j in range(3):
+            if first and j < 2:
+                for p in range(pairs):
+                    ld_qkv[j * pairs + p].wait()
+            for p in range(pairs):
+                if first and j == 2:
+                    ld_qkv[j * pairs + p].wait()
+                project(j, p)
+            if first and j == 0:
+                load_out()
+                ld_tk.wait()
+                for h in range(heads):
+                    text_head(h)
+            if first and j == 1:
+                ld_fin.wait()
+                final_weights()
+            if j == (1 if first else 2):
+                norm_heads(q_s, q_n)
+                norm_heads(k_s, k_n)
+                for h in range(heads):
+                    score(h)
         if first:
-            for p in range(pairs):
-                ld_qkv[p].wait()
-                project(0, p)
-                if p == 0:
-                    ld_tk.wait()
-                for h in (2 * p, 2 * p + 1):
-                    text_head(h)
-            norm_heads(q_s, q_n)
-            for p in range(pairs):
-                ld_qkv[pairs + p].wait()
-                project(1, p)
-                if p == 0:
-                    ld_fin.wait()
-                    final_weights()
-            norm_heads(k_s, k_n)
-            for h in range(heads):
-                score(h)
-            for p in range(pairs):
-                ld_qkv[2 * pairs + p].wait()
-                project(2, p)
             ld_tv.wait()
-        else:
-            for j in range(3):
-                for p in range(pairs):
-                    project(j, p)
-            norm_heads(q_s, q_n)
-            norm_heads(k_s, k_n)
-            for h in range(heads):
-                score(h)
         for p in range(pairs):
             for h in (2 * p, 2 * p + 1):
                 weigh(h)
@@ -497,7 +493,7 @@
             dma((ITERS, steps)),
         ],
         compiler_params=pltpu.CompilerParams(
-            collective_id=0, has_side_effects=True, vmem_limit_bytes=56 * 2**20
+            collective_id=0, has_side_effects=True, vmem_limit_bytes=55193 * 1024
         ),
         cost_estimate=pl.CostEstimate(
             flops=5 * 10**9, bytes_accessed=25 * 10**6, transcendentals=10**6

time: 33.7 us -> 31.9 us (0.947)
  Pallas kernels: 30.8 us -> 29.8 us
  local copies, waits for them, and re-layouts: 1.38 us -> 0.62 us
    pallas_call x1, Pallas kernels: 30.8 us -> 29.8 us  [per_device(): pl.pallas_call(functools.partial(kernel, groups, steps), out_shape=jax.Sh...]
    unnamed x1, local copies, waits for them, and re-layouts: 1.38 us -> 0.62 us
where the time goes in v4:
time: 31.9 us; the launch traced here: 31.8 us
  Pallas kernels  29.8 us (93%)
  between operations  1.3 us (4%)
  local copies, waits for them, and re-layouts  0.62 us (2%)
    pallas_call x1, Pallas kernels, per_device(): pl.pallas_call(functools.partial(kernel, groups, steps), out_shape=jax.Sh...  29.8 us

profile of v4, /device:TPU:226, one launch (start us, length us, event | category | flops | bytes accessed | tf_op | source)
XLA Modules:
  0.0 31.8 jit_solution(15219741646743237143)
XLA Ops:
  1.3 29.8 %picard.1 = f32[64,64]{1,0:T(8,128)S(1)} custom-call(f32[1]{0:T(128)S(6)} %copy.12.step_size_hbm, s32[1]{0:T(128)S(6)} %copy.13.step_ids_hbm, f32[8,64,64]{2,1,0:T(8,128)} %noise_hbm.1, f32[3,50,3072]{2,1,0:T(8,128)} %bitcast.6, bf16[64,3072]{1,0:T(8,128)(2,1)} %w_in_hbm.1, bf16[3,3072,768]{2,1,0:T(8,128)(2,1)} %bitcast.5, bf16[1536,3072]{1,0:T(8,128)(2,1)} %w_out_hbm.1, ...), custom_call_target="tpu_custom_call" | custom-call | flops 5000000000 | bytes 25000000 | tf_op jit(solution)/shard_map/picard/pallas_call | solution.py:443
  31.1 0.6 %copy.14 = f32[1,64,64]{2,1,0:T(8,128)} copy(f32[1,64,64]{2,1,0:T(8,128)S(1)} %bitcast.4) | data formatting | bytes 32768

commit v5 on v4

--- a/solution.py
+++ b/solution.py
@@ -119,10 +119,9 @@
     ld_in = load(w_in_hbm, w_in2.at[pl.ds(0, chan)])
     ld_mod = load(mod_hbm.at[pl.ds(0, 2)], mod_v)
     ld_tk = load(tk_hbm, tk)
+    ld_fin = load(w_fin_hbm, w_fin)
     ld_qkv = []
     for j in range(3):
-        if j == 1:
-            ld_fin = load(w_fin_hbm, w_fin)
         if j == 2:
             ld_tv = load(tv_hbm, tv)
             ld_gate = load(mod_hbm.at[2], gate_v)
@@ -296,24 +295,24 @@
         embed(1)
         modulate(1)
         lat_move.wait_send()
+        if first:
+            ld_tk.wait()
+            for h in range(heads):
+                text_head(h)
+            ld_fin.wait()
+            final_weights()
         for j in range(3):
-            if first and j < 2:
+            if first:
                 for p in range(pairs):
                     ld_qkv[j * pairs + p].wait()
             for p in range(pairs):
-                if first and j == 2:
-                    ld_qkv[j * pairs + p].wait()
                 project(j, p)
             if first and j == 0:
                 load_out()
-                ld_tk.wait()
-                for h in range(heads):
-                    text_head(h)
-            if first and j == 1:
-                ld_fin.wait()
-                final_weights()
+                norm_heads(q_s, q_n)
             if j == (1 if first else 2):
-                norm_heads(q_s, q_n)
+                if not first:
+                    norm_heads(q_s, q_n)
                 norm_heads(k_s, k_n)
                 for h in range(heads):
                     score(h)
@@ -344,28 +343,30 @@
             gate = gate_b[0:1, there]
             mixed[:, cs] = hidden[:, there] + gate * (proj[:, cs] + from_par)
 
-        for r0 in range(0, rows, 16):
-            rs = pl.ds(r0, 16)
-            m = mixed[rs, :]
-            mean = jnp.sum(m, axis=-1, keepdims=True) * (1.0 / half)
-            c = m - mean
-            square = jnp.sum(c * c, axis=-1, keepdims=True)
-            centred[rs, :] = c.astype(BF16)
-            dst = u_mine if r0 < tok else u_send
-            ds = pl.ds(r0 % tok, 16)
-            dst[1, ds, :] = jnp.broadcast_to(mean, (16, 2 * chan))
-            dst[2, ds, :] = jnp.broadcast_to(square, (16, 2 * chan))
-        u = jnp.dot(centred[...], w_fin_t[...], preferred_element_type=F32)
-        u_mine[0] = u[0:tok]
-        u_send[0] = u[tok:rows]
-        if first:
-
-            @pl.when(s == 0)
-            def _():
-                pl.semaphore_wait(barrier, steps - 1)
-
-            ld_size.wait()
-        u_move.start()
+        for part in (1, 0):
+            dst = (u_mine, u_send)[part]
+            for r0 in range(0, tok, 16):
+                rs = pl.ds(part * tok + r0, 16)
+                m = mixed[rs, :]
+                mean = jnp.sum(m, axis=-1, keepdims=True) * (1.0 / half)
+                c = m - mean
+                square = jnp.sum(c * c, axis=-1, keepdims=True)
+                centred[rs, :] = c.astype(BF16)
+                ds = pl.ds(r0, 16)
+                dst[1, ds, :] = jnp.broadcast_to(mean, (16, 2 * chan))
+                dst[2, ds, :] = jnp.broadcast_to(square, (16, 2 * chan))
+            dst[0] = jnp.dot(
+                centred[pl.ds(part * tok, tok), :], w_fin_t[...], preferred_element_type=F32
+            )
+            if part == 1:
+                if first:
+
+                    @pl.when(s == 0)
+                    def _():
+                        pl.semaphore_wait(barrier, steps - 1)
+
+                    ld_size.wait()
+                u_move.start()
         u_move.wait()
         delta = (u_mine[1] - u_recv[1]) * 0.5
         var = (u_mine[2] + u_recv[2]) * (1.0 / width) + delta * delta

time: 31.9 us -> 31 us (0.972)
  Pallas kernels: 29.8 us -> 28.9 us
    pallas_call x1, Pallas kernels: 29.8 us -> 28.9 us  [per_device(): pl.pallas_call(functools.partial(kernel, groups, steps), out_shape=jax.Sh...]
where the time goes in v5:
time: 31 us; the launch traced here: 30.8 us
  Pallas kernels  28.9 us (93%)
  between operations  1.3 us (4%)
  local copies, waits for them, and re-layouts  0.62 us (2%)
    pallas_call x1, Pallas kernels, per_device(): pl.pallas_call(functools.partial(kernel, groups, steps), out_shape=jax.Sh...  28.9 us

profile of v5, /device:TPU:226, one launch (start us, length us, event | category | flops | bytes accessed | tf_op | source)
XLA Modules:
  0.0 30.8 jit_solution(17793361949767431993)
XLA Ops:
  1.3 28.9 %picard.1 = f32[64,64]{1,0:T(8,128)S(1)} custom-call(f32[1]{0:T(128)S(6)} %copy.12.step_size_hbm, s32[1]{0:T(128)S(6)} %copy.13.step_ids_hbm, f32[8,64,64]{2,1,0:T(8,128)} %noise_hbm.1, f32[3,50,3072]{2,1,0:T(8,128)} %bitcast.6, bf16[64,3072]{1,0:T(8,128)(2,1)} %w_in_hbm.1, bf16[3,3072,768]{2,1,0:T(8,128)(2,1)} %bitcast.5, bf16[1536,3072]{1,0:T(8,128)(2,1)} %w_out_hbm.1, ...), custom_call_target="tpu_custom_call" | custom-call | flops 5000000000 | bytes 25000000 | tf_op jit(solution)/shard_map/picard/pallas_call | solution.py:444
  30.2 0.6 %copy.14 = f32[1,64,64]{2,1,0:T(8,128)} copy(f32[1,64,64]{2,1,0:T(8,128)S(1)} %bitcast.4) | data formatting | bytes 32768
